TPU v7x, 512 devices: a whole 4x4x16 slice. The times are simulated.
512 devices in a mesh: samp: 16 (over z), var: 32 (over x, y, core).
Axes of the slice: x: 4, y: 4, z: 16, core: 2. Of those that a mesh axis runs over, the one named last changes fastest.
Arguments:
- dosage: bfloat16 [3072, 32768], P('samp', 'var'), may hold values from -5 to 5
- coefficients: bfloat16 [32768, 256], P('var'), as said below
- targets: bfloat16 [3072, 256], P('samp'), may hold values from -5 to 5
- mask_words: int32 [3072, 16], P('samp'), may hold values from 0 to 65535
- penalty: float32 [256], replicated, may hold values from 0.1 to 1.5
- past_steps: bfloat16 [8, 32768, 256], P(None, ('var', 'samp')), as said below
- past_changes: bfloat16 [8, 32768, 256], P(None, ('var', 'samp')), as said below
Outputs:
- updated: float32 [32768, 256], P(('var', 'samp'))
Inputs may be any that keep to these rules, and one draw needn't show every extreme that they name: `past_changes`: each stored change y_i has a positive inner product with its own step s_i. `past_steps`: steps and changes come as pairs drawn together. The coefficients are drawn together with the stored pairs.
All inputs are finite; a program needn't handle non-finite values.
Results may differ from a plain program's by a relative error of at most 0.00066.
Values may be sent and summed in bfloat16 or wider, within the bound.
A program may use at most 64 MiB of HBM per device.

v0:
```python
import jax
import jax.numpy as jnp
from jax import lax
from jax.sharding import PartitionSpec as P

step_size = 0.5


def unpack_mask(mask_words):
    shifts = jnp.arange(16, dtype=jnp.int32)
    flags = jnp.bitwise_and(jnp.right_shift(mask_words[:, :, None], shifts[None, None, :]), 1)
    return flags.reshape(mask_words.shape[0], -1).astype(jnp.float32)


def recursive_apply(gradient, past_steps, past_changes):
    count = past_steps.shape[0]
    pair_local = jnp.einsum(
        "mvk,mvk->m", past_steps, past_changes, preferred_element_type=jnp.float32
    )
    last_change = past_changes[count - 1].astype(jnp.float32)
    last_local = jnp.sum(last_change * last_change)
    pair_dots, last_norm = lax.psum((pair_local, last_local), ("samp", "var"))
    scaling = pair_dots[count - 1] / last_norm
    running = gradient
    forward_weights = [None] * count
    for i in reversed(range(count)):
        step_wide = past_steps[i].astype(jnp.float32)
        product = lax.psum(jnp.sum(step_wide * running), ("samp", "var"))
        forward_weights[i] = product / pair_dots[i]
        running = running - forward_weights[i] * past_changes[i].astype(jnp.float32)
    running = scaling * running
    for i in range(count):
        change_wide = past_changes[i].astype(jnp.float32)
        product = lax.psum(jnp.sum(change_wide * running), ("samp", "var"))
        running = running + (forward_weights[i] - product / pair_dots[i]) * past_steps[i].astype(
            jnp.float32
        )
    return running


def per_device(dosage, coefficients, targets, mask_words, penalty, past_steps, past_changes):
    var_count = lax.axis_size("var")
    scale = (dosage.shape[1] * var_count) ** (-0.5)
    observed = unpack_mask(mask_words)
    margin = (
        lax.psum(jnp.dot(dosage, coefficients, preferred_element_type=jnp.float32), "var") * scale
    )
    residual = (observed * (margin - targets.astype(jnp.float32))).astype(jnp.bfloat16)
    owned_count = dosage.shape[1] // lax.axis_size("samp")
    gradient = (
        lax.psum_scatter(
            lax.dot_general(
                dosage, residual, (((0,), (0,)), ((), ())), preferred_element_type=jnp.float32
            ),
            "samp",
            scatter_dimension=0,
            tiled=True,
        )
        * scale
    )
    direction = recursive_apply(gradient, past_steps, past_changes)
    first_owned = lax.axis_index("samp") * owned_count
    owned_coefs = lax.dynamic_slice_in_dim(coefficients, first_owned, owned_count, 0).astype(
        jnp.float32
    )
    moved = owned_coefs - step_size * direction
    limit = step_size * penalty[None, :]
    return moved - jnp.clip(moved, -limit, limit)


def solution(mesh):
    in_specs = (
        P("samp", "var"),
        P("var", None),
        P("samp", None),
        P("samp", None),
        P(),
        P(None, ("var", "samp"), None),
        P(None, ("var", "samp"), None),
    )
    out_specs = P(("var", "samp"), None)
    return jax.shard_map(
        per_device, mesh=mesh, in_specs=in_specs, out_specs=out_specs, check_vma=False
    )
```

profile of v0, /device:TPU:1, one launch (start us, length us, event | category | flops | bytes accessed | tf_op | source)
XLA Modules:
  0.0 1859.9 jit_solution(4022741216258788676)
XLA Ops:
  6.5 1.0 copy-done
  7.6 1.9 fusion.52
  9.6 0.6 copy-done.5
  10.5 135.3 %all-reduce.4.cloned.1.call-done = f32[192,256]{1,0:T(8,128)} async-done(((f32[192,256]{1,0:T(8,128)}), f32[192,256]{1,0:T(8,128)}) %all-reduce.4.cloned.1.call-update) | async-done | bytes 196624 | tf_op jit(solution)/shard_map/psum | solution.py:46
  145.8 1.3 convolution_bitcast_fusion
  147.0 1.3 copy.72
  148.4 0.9 copy-done.3
  149.5 0.8 copy-done.2
  150.4 0.1 copy.77
  152.1 0.2 fusion
  152.3 0.5 copy-done.6
  152.8 56.1 %reduce-scatter.4.cloned.1.call-done = f32[64,256]{1,0:T(8,128)} async-done(((f32[1024,256]{1,0:T(8,128)}), f32[64,256]{1,0:T(8,128)}) %reduce-scatter.4.cloned.1.call-update) | async-done | bytes 65552
  208.9 0.9 copy.73
  209.8 0.6 fusion.30
  210.5 111.4 %all-reduce.1 = (f32[]{:T(128)}, f32[8]{0:T(128)S(1)}) all-reduce(f32[]{:T(128)} %fusion.30, f32[8]{0:T(128)S(1)} %fusion), channel_id=1, replica_groups=mesh['samp'=16,'var'=32] {'samp','var'}, use_global_device_ids=true, to_apply=%region_6.0 | all-reduce | flops 9 | bytes 72 | tf_op jit(solution)/shard_map/psum | solution.py:28
  321.9 0.7 fusion.51
  323.9 0.6 fusion.28
  324.6 99.9 %psum.137 = f32[]{:T(128)} all-reduce(f32[]{:T(128)} %fusion.28), channel_id=1, replica_groups=mesh['samp'=16,'var'=32] {'samp','var'}, use_global_device_ids=true, to_apply=%region_8.0 | all-reduce | flops 1 | bytes 8 | tf_op jit(solution)/shard_map/psum | solution.py:28
  425.7 0.7 fusion.34
  426.3 100.5 %psum.138 = f32[]{:T(128)} all-reduce(f32[]{:T(128)} %get-tuple-element.6), channel_id=1, replica_groups=mesh['samp'=16,'var'=32] {'samp','var'}, use_global_device_ids=true, to_apply=%region_10.0 | all-reduce | flops 1 | bytes 8 | tf_op jit(solution)/shard_map/psum | solution.py:28
  528.2 0.7 fusion.20
  528.9 99.2 %psum.139 = f32[]{:T(128)} all-reduce(f32[]{:T(128)} %get-tuple-element.21), channel_id=1, replica_groups=mesh['samp'=16,'var'=32] {'samp','var'}, use_global_device_ids=true, to_apply=%region_12.0 | all-reduce | flops 1 | bytes 8 | tf_op jit(solution)/shard_map/psum | solution.py:28
  629.4 0.6 fusion.16
  630.0 100.2 %psum.140 = f32[]{:T(128)} all-reduce(f32[]{:T(128)} %fusion.16), channel_id=1, replica_groups=mesh['samp'=16,'var'=32] {'samp','var'}, use_global_device_ids=true, to_apply=%region_14.0 | all-reduce | flops 1 | bytes 8 | tf_op jit(solution)/shard_map/psum | solution.py:28
  731.5 0.6 fusion.12
  732.1 99.3 %psum.141 = f32[]{:T(128)} all-reduce(f32[]{:T(128)} %get-tuple-element.19), channel_id=1, replica_groups=mesh['samp'=16,'var'=32] {'samp','var'}, use_global_device_ids=true, to_apply=%region_16.0 | all-reduce | flops 1 | bytes 8 | tf_op jit(solution)/shard_map/psum | solution.py:28
  832.8 0.6 fusion.8
  833.5 100.2 %psum.142 = f32[]{:T(128)} all-reduce(f32[]{:T(128)} %fusion.8), channel_id=1, replica_groups=mesh['samp'=16,'var'=32] {'samp','var'}, use_global_device_ids=true, to_apply=%region_18.0 | all-reduce | flops 1 | bytes 8 | tf_op jit(solution)/shard_map/psum | solution.py:28
  934.9 0.6 fusion.4
  935.5 99.5 %all-reduce = (f32[]{:T(128)}, f32[]{:T(128)}) all-reduce(f32[]{:T(128)} %get-tuple-element.17, f32[]{:T(128)} %get-tuple-element.5), channel_id=1, replica_groups=mesh['samp'=16,'var'=32] {'samp','var'}, use_global_device_ids=true, to_apply=%region_20.0 | all-reduce | flops 2 | bytes 16 | tf_op jit(solution)/shard_map/psum | solution.py:28
  1037.8 0.6 fusion.3
  1038.4 100.2 %psum.144 = f32[]{:T(128)} all-reduce(f32[]{:T(128)} %fusion.3), channel_id=1, replica_groups=mesh['samp'=16,'var'=32] {'samp','var'}, use_global_device_ids=true, to_apply=%region_22.0 | all-reduce | flops 1 | bytes 8 | tf_op jit(solution)/shard_map/psum | solution.py:34
  1140.0 0.7 fusion.7
  1140.7 99.4 %psum.145 = f32[]{:T(128)} all-reduce(f32[]{:T(128)} %get-tuple-element.15), channel_id=1, replica_groups=mesh['samp'=16,'var'=32] {'samp','var'}, use_global_device_ids=true, to_apply=%region_24.0 | all-reduce | flops 1 | bytes 8 | tf_op jit(solution)/shard_map/psum | solution.py:34
  1241.3 0.6 fusion.11
  1242.0 100.2 %psum.146 = f32[]{:T(128)} all-reduce(f32[]{:T(128)} %fusion.11), channel_id=1, replica_groups=mesh['samp'=16,'var'=32] {'samp','var'}, use_global_device_ids=true, to_apply=%region_26.0 | all-reduce | flops 1 | bytes 8 | tf_op jit(solution)/shard_map/psum | solution.py:34
  1343.5 0.6 fusion.15
  1344.1 99.6 %psum.147 = f32[]{:T(128)} all-reduce(f32[]{:T(128)} %fusion.15), channel_id=1, replica_groups=mesh['samp'=16,'var'=32] {'samp','var'}, use_global_device_ids=true, to_apply=%region_28.0 | all-reduce | flops 1 | bytes 8 | tf_op jit(solution)/shard_map/psum | solution.py:34
  1445.0 0.7 fusion.19
  1445.7 100.2 %psum.148 = f32[]{:T(128)} all-reduce(f32[]{:T(128)} %get-tuple-element.13), channel_id=1, replica_groups=mesh['samp'=16,'var'=32] {'samp','var'}, use_global_device_ids=true, to_apply=%region_30.0 | all-reduce | flops 1 | bytes 8 | tf_op jit(solution)/shard_map/psum | solution.py:34
  1547.2 0.6 fusion.23
  1547.8 99.4 %psum.149 = f32[]{:T(128)} all-reduce(f32[]{:T(128)} %fusion.23), channel_id=1, replica_groups=mesh['samp'=16,'var'=32] {'samp','var'}, use_global_device_ids=true, to_apply=%region_32.0 | all-reduce | flops 1 | bytes 8 | tf_op jit(solution)/shard_map/psum | solution.py:34
  1648.5 0.6 fusion.27
  1649.2 100.2 %psum.150 = f32[]{:T(128)} all-reduce(f32[]{:T(128)} %get-tuple-element.11), channel_id=1, replica_groups=mesh['samp'=16,'var'=32] {'samp','var'}, use_global_device_ids=true, to_apply=%region_34.0 | all-reduce | flops 1 | bytes 8 | tf_op jit(solution)/shard_map/psum | solution.py:34
  1750.6 0.6 fusion.36
  1751.4 99.4 %psum.151 = f32[]{:T(128)} all-reduce(f32[]{:T(128)} %fusion.36), channel_id=1, replica_groups=mesh['samp'=16,'var'=32] {'samp','var'}, use_global_device_ids=true, to_apply=%region_36.0 | all-reduce | flops 1 | bytes 8 | tf_op jit(solution)/shard_map/psum | solution.py:34
  1852.2 0.1 minimum_subtract_fusion
  1852.3 0.7 copy.64
  (37 shorter events, 2.2 us)
Async XLA Ops:
  6.5 1.0 copy-start
  6.5 139.2 %all-reduce.4.cloned.1.call-start = ((), (), s32[]{:S(2)}) async-start(), calls=%async_computation.1 | async-start | bytes 393216 | tf_op jit(solution)/shard_map/psum | solution.py:46
  9.5 0.7 copy-start.5
  9.5 136.2 %copy-start.1 = (bf16[192,1024]{1,0:T(8,128)(2,1)S(1)}, bf16[192,1024]{1,0:T(8,128)(2,1)}, u32[]{:S(2)}) copy-start(bf16[192,1024]{1,0:T(8,128)(2,1)} %param.7) | copy-start | bytes 1179652
  9.6 199.3 %reduce-scatter.4.cloned.1.call-start = ((), (), s32[]{:S(2)}) async-start(), calls=%async_computation.2 | async-start | bytes 1114112
  10.3 135.5 %copy-start.4 = (bf16[192,256]{1,0:T(8,128)(2,1)S(1)}, bf16[192,256]{1,0:T(8,128)(2,1)}, u32[]{:S(2)}) copy-start(bf16[192,256]{1,0:T(8,128)(2,1)} %param.9) | copy-start | bytes 294916
  148.4 0.9 copy-start.3
  149.3 0.9 copy-start.2
  152.1 0.7 copy-start.6
Sparse Core Ops, SparseCore 0:
  10.6 135.1 all-reduce.3
  148.8 60.0 reduce-scatter.3
where the time goes:
time: 1860 us
  blocking collectives  1610 us (87%)
  waiting for transfers between devices  191 us (10%)
  between operations  36 us (2%)
    psum x8, blocking collectives, recursive_apply(): product = lax.psum(jnp.sum(step_wide * running), ('samp', 'var'))  810 us
    psum x8, blocking collectives, recursive_apply(): product = lax.psum(jnp.sum(change_wide * running), ('samp', 'var'))  799 us
    psum x1, waiting for transfers between devices, per_device(): lax.psum(jnp.dot(dosage, coefficients, preferred_element_type=jnp.float32...  135 us
    unnamed x3, waiting for transfers between devices  56.1 us
  transfers between devices with their start and end apart: 2, of which 2 were waited for; matrix products, arithmetic and copies ran while one was open for 0% of the time, Pallas kernels for 0%

commit v1 on v0

--- a/solution.py
+++ b/solution.py
@@ -43,7 +43,13 @@
     scale = (dosage.shape[1] * var_count) ** (-0.5)
     observed = unpack_mask(mask_words)
     margin = (
-        lax.psum(jnp.dot(dosage, coefficients, preferred_element_type=jnp.float32), "var") * scale
+        jnp.sum(
+            lax.all_gather(
+                jnp.dot(dosage, coefficients, preferred_element_type=jnp.float32), "var"
+            ),
+            axis=0,
+        )
+        * scale
     )
     residual = (observed * (margin - targets.astype(jnp.float32))).astype(jnp.bfloat16)
     owned_count = dosage.shape[1] // lax.axis_size("samp")

time: 1860 us -> 1800 us (0.968)
  waiting for transfers between devices: 191 us -> 127 us
    psum x1 -> x0, waiting for transfers between devices: 135 us -> none  [per_device(): lax.psum(jnp.dot(dosage, coefficients, preferred_element_type=jnp.float32...]
    all_gather x0 -> x1, waiting for transfers between devices: none -> 70.1 us  [per_device(): lax.all_gather(jnp.dot(dosage, coefficients, preferred_element_type=jnp.f...]
where the time goes in v1:
time: 1800 us
  blocking collectives  1610 us (89%)
  waiting for transfers between devices  127 us (7%)
  between operations  36 us (2%)
    psum x8, blocking collectives, recursive_apply(): product = lax.psum(jnp.sum(step_wide * running), ('samp', 'var'))  811 us
    psum x8, blocking collectives, recursive_apply(): product = lax.psum(jnp.sum(change_wide * running), ('samp', 'var'))  799 us
    all_gather x1, waiting for transfers between devices, per_device(): lax.all_gather(jnp.dot(dosage, coefficients, preferred_element_type=jnp.f...  70.1 us
    unnamed x3, waiting for transfers between devices  57.2 us
  transfers between devices with their start and end apart: 2, of which 2 were waited for; matrix products, arithmetic and copies ran while one was open for 0% of the time, Pallas kernels for 0%

profile of v1, /device:TPU:1, one launch (start us, length us, event | category | flops | bytes accessed | tf_op | source)
XLA Modules:
  0.0 1796.8 jit_solution(12799716501920456168)
XLA Ops:
  6.5 1.0 copy-done
  7.6 1.9 fusion.52
  9.7 0.7 shift_right_arithmetic.20
  10.5 70.1 %all-gather.3.cloned.1.call-done = f32[6144,256]{1,0:T(8,128)} async-done(((f32[192,256]{1,0:T(8,128)}), f32[6144,256]{1,0:T(8,128)}) %all-gather.3.cloned.1.call-update) | async-done | bytes 6291472 | tf_op jit(solution)/shard_map/all_gather | solution.py:47
  80.7 3.2 reduce_sum.163
  83.9 0.3 convolution_bitcast_fusion
  84.3 1.3 copy.72
  85.8 0.1 copy.85
  85.9 0.1 copy.81
  86.0 0.1 copy.77
  87.3 0.2 fusion
  87.5 57.2 %reduce-scatter.4.cloned.1.call-done = f32[64,256]{1,0:T(8,128)} async-done(((f32[1024,256]{1,0:T(8,128)}), f32[64,256]{1,0:T(8,128)}) %reduce-scatter.4.cloned.1.call-update) | async-done | bytes 65552
  144.7 0.9 copy.73
  145.6 0.6 fusion.30
  146.4 111.6 %all-reduce.1 = (f32[]{:T(128)}, f32[8]{0:T(128)S(1)}) all-reduce(f32[]{:T(128)} %fusion.30, f32[8]{0:T(128)S(1)} %fusion), channel_id=1, replica_groups=mesh['samp'=16,'var'=32] {'samp','var'}, use_global_device_ids=true, to_apply=%region_6.0 | all-reduce | flops 9 | bytes 72 | tf_op jit(solution)/shard_map/psum | solution.py:28
  258.0 0.7 fusion.51
  260.1 0.6 fusion.28
  260.8 100.0 %psum.129 = f32[]{:T(128)} all-reduce(f32[]{:T(128)} %fusion.28), channel_id=1, replica_groups=mesh['samp'=16,'var'=32] {'samp','var'}, use_global_device_ids=true, to_apply=%region_8.0 | all-reduce | flops 1 | bytes 8 | tf_op jit(solution)/shard_map/psum | solution.py:28
  362.0 0.7 fusion.34
  362.7 100.5 %psum.130 = f32[]{:T(128)} all-reduce(f32[]{:T(128)} %get-tuple-element.6), channel_id=1, replica_groups=mesh['samp'=16,'var'=32] {'samp','var'}, use_global_device_ids=true, to_apply=%region_10.0 | all-reduce | flops 1 | bytes 8 | tf_op jit(solution)/shard_map/psum | solution.py:28
  464.5 0.7 fusion.20
  465.2 99.3 %psum.131 = f32[]{:T(128)} all-reduce(f32[]{:T(128)} %get-tuple-element.21), channel_id=1, replica_groups=mesh['samp'=16,'var'=32] {'samp','var'}, use_global_device_ids=true, to_apply=%region_12.0 | all-reduce | flops 1 | bytes 8 | tf_op jit(solution)/shard_map/psum | solution.py:28
  565.8 0.6 fusion.16
  566.6 100.3 %psum.132 = f32[]{:T(128)} all-reduce(f32[]{:T(128)} %fusion.16), channel_id=1, replica_groups=mesh['samp'=16,'var'=32] {'samp','var'}, use_global_device_ids=true, to_apply=%region_14.0 | all-reduce | flops 1 | bytes 8 | tf_op jit(solution)/shard_map/psum | solution.py:28
  668.1 0.6 fusion.12
  668.8 99.5 %psum.133 = f32[]{:T(128)} all-reduce(f32[]{:T(128)} %get-tuple-element.19), channel_id=1, replica_groups=mesh['samp'=16,'var'=32] {'samp','var'}, use_global_device_ids=true, to_apply=%region_16.0 | all-reduce | flops 1 | bytes 8 | tf_op jit(solution)/shard_map/psum | solution.py:28
  769.6 0.6 fusion.8
  770.3 100.1 %psum.134 = f32[]{:T(128)} all-reduce(f32[]{:T(128)} %fusion.8), channel_id=1, replica_groups=mesh['samp'=16,'var'=32] {'samp','var'}, use_global_device_ids=true, to_apply=%region_18.0 | all-reduce | flops 1 | bytes 8 | tf_op jit(solution)/shard_map/psum | solution.py:28
  871.5 0.6 fusion.4
  872.2 99.7 %all-reduce = (f32[]{:T(128)}, f32[]{:T(128)}) all-reduce(f32[]{:T(128)} %get-tuple-element.17, f32[]{:T(128)} %get-tuple-element.5), channel_id=1, replica_groups=mesh['samp'=16,'var'=32] {'samp','var'}, use_global_device_ids=true, to_apply=%region_20.0 | all-reduce | flops 2 | bytes 16 | tf_op jit(solution)/shard_map/psum | solution.py:28
  974.7 0.6 fusion.3
  975.3 100.0 %psum.136 = f32[]{:T(128)} all-reduce(f32[]{:T(128)} %fusion.3), channel_id=1, replica_groups=mesh['samp'=16,'var'=32] {'samp','var'}, use_global_device_ids=true, to_apply=%region_22.0 | all-reduce | flops 1 | bytes 8 | tf_op jit(solution)/shard_map/psum | solution.py:34
  1076.7 0.7 fusion.7
  1077.4 99.6 %psum.137 = f32[]{:T(128)} all-reduce(f32[]{:T(128)} %get-tuple-element.15), channel_id=1, replica_groups=mesh['samp'=16,'var'=32] {'samp','var'}, use_global_device_ids=true, to_apply=%region_24.0 | all-reduce | flops 1 | bytes 8 | tf_op jit(solution)/shard_map/psum | solution.py:34
  1178.2 0.6 fusion.11
  1178.8 100.2 %psum.138 = f32[]{:T(128)} all-reduce(f32[]{:T(128)} %fusion.11), channel_id=1, replica_groups=mesh['samp'=16,'var'=32] {'samp','var'}, use_global_device_ids=true, to_apply=%region_26.0 | all-reduce | flops 1 | bytes 8 | tf_op jit(solution)/shard_map/psum | solution.py:34
  1280.4 0.6 fusion.15
  1281.0 99.5 %psum.139 = f32[]{:T(128)} all-reduce(f32[]{:T(128)} %fusion.15), channel_id=1, replica_groups=mesh['samp'=16,'var'=32] {'samp','var'}, use_global_device_ids=true, to_apply=%region_28.0 | all-reduce | flops 1 | bytes 8 | tf_op jit(solution)/shard_map/psum | solution.py:34
  1381.8 0.7 fusion.19
  1382.5 100.1 %psum.140 = f32[]{:T(128)} all-reduce(f32[]{:T(128)} %get-tuple-element.13), channel_id=1, replica_groups=mesh['samp'=16,'var'=32] {'samp','var'}, use_global_device_ids=true, to_apply=%region_30.0 | all-reduce | flops 1 | bytes 8 | tf_op jit(solution)/shard_map/psum | solution.py:34
  1483.9 0.6 fusion.23
  1484.6 99.5 %psum.141 = f32[]{:T(128)} all-reduce(f32[]{:T(128)} %fusion.23), channel_id=1, replica_groups=mesh['samp'=16,'var'=32] {'samp','var'}, use_global_device_ids=true, to_apply=%region_32.0 | all-reduce | flops 1 | bytes 8 | tf_op jit(solution)/shard_map/psum | solution.py:34
  1585.4 0.6 fusion.27
  1586.0 100.1 %psum.142 = f32[]{:T(128)} all-reduce(f32[]{:T(128)} %get-tuple-element.11), channel_id=1, replica_groups=mesh['samp'=16,'var'=32] {'samp','var'}, use_global_device_ids=true, to_apply=%region_34.0 | all-reduce | flops 1 | bytes 8 | tf_op jit(solution)/shard_map/psum | solution.py:34
  1687.4 0.6 fusion.36
  1688.1 99.5 %psum.143 = f32[]{:T(128)} all-reduce(f32[]{:T(128)} %fusion.36), channel_id=1, replica_groups=mesh['samp'=16,'var'=32] {'samp','var'}, use_global_device_ids=true, to_apply=%region_36.0 | all-reduce | flops 1 | bytes 8 | tf_op jit(solution)/shard_map/psum | solution.py:34
  1789.1 0.1 minimum_subtract_fusion
  1789.2 0.7 copy.64
  (36 shorter events, 1.9 us)
Async XLA Ops:
  6.5 1.0 copy-start
  6.5 77.4 %copy-start.1 = (bf16[192,1024]{1,0:T(8,128)(2,1)S(1)}, bf16[192,1024]{1,0:T(8,128)(2,1)}, u32[]{:S(2)}) copy-start(bf16[192,1024]{1,0:T(8,128)(2,1)} %param.7) | copy-start | bytes 1179652
  6.5 77.4 %copy-start.4 = (bf16[192,256]{1,0:T(8,128)(2,1)S(1)}, bf16[192,256]{1,0:T(8,128)(2,1)}, u32[]{:S(2)}) copy-start(bf16[192,256]{1,0:T(8,128)(2,1)} %param.9) | copy-start | bytes 294916
  6.5 74.1 %all-gather.3.cloned.1.call-start = ((), (), s32[]{:S(2)}) async-start(), calls=%async_computation.1 | async-start | bytes 6488064 | tf_op jit(solution)/shard_map/all_gather | solution.py:47
  9.5 76.1 %copy-start.3 = (bf16[8,64,256]{2,1,0:T(8,128)(2,1)S(1)}, bf16[8,64,256]{2,1,0:T(8,128)(2,1)}, u32[]{:S(2)}) copy-start(bf16[8,64,256]{2,1,0:T(8,128)(2,1)} %param.12) | copy-start | bytes 786436
  9.5 135.1 %reduce-scatter.4.cloned.1.call-start = ((), (), s32[]{:S(2)}) async-start(), calls=%async_computation.2 | async-start | bytes 1114112
  80.7 6.0 copy-start.2
  80.7 6.8 copy-start.5
Sparse Core Ops, SparseCore 0:
  10.5 70.1 all-gather.2
  85.7 58.8 reduce-scatter.3
